TPU v7x, 256 devices: a whole 4x4x8 slice. The times are simulated.
256 devices in a mesh: row: 64 (over z, y, core), tm: 4 (over x).
Axes of the slice: x: 4, y: 4, z: 8, core: 2. Of those that a mesh axis runs over, the one named last changes fastest.
Arguments:
- snapshots: float32 [524288, 512], P('row', 'tm'), may hold values from -16 to 16
- modes: float32 [524288, 32], P('row'), may hold values from -6 to 6
- ridge: float32 [528], replicated, may hold values from 0.0005 to 0.005
Outputs:
- correction: float32 [524288, 528], P(('row', 'tm'))
All inputs are finite; a program needn't handle non-finite values.
Results may differ from a plain program's by a relative error of at most 0.0003.
Values sent between devices are 32-bit elements; how exact they have to be, the bound alone decides.
A program may use at most 128 MiB of HBM per device.

v0:
```python
import jax
import jax.numpy as jnp
import numpy as np
from jax import lax
from jax.sharding import PartitionSpec as P

R = 32


def quad_features(coords):
    first, second = np.triu_indices(R)
    return coords[first] * coords[second]


def small_factor(block):
    high = lax.Precision.HIGHEST
    width = block.shape[0]
    places = jnp.arange(width, dtype=jnp.int32)

    def column_step(index, lower):
        pick = (places == index).astype(jnp.float32)
        row_here = jnp.dot(pick, lower, precision=high)
        column = jnp.dot(block, pick, precision=high) - jnp.dot(lower, row_here, precision=high)
        pivot = jnp.sqrt(jnp.dot(column, pick, precision=high))
        scaled = jnp.where(places >= index, column / pivot, 0.0)
        return lower + scaled[:, None] * pick[None, :]

    return lax.fori_loop(0, width, column_step, jnp.zeros_like(block))


def small_inverse(lower):
    high = lax.Precision.HIGHEST
    width = lower.shape[0]
    places = jnp.arange(width, dtype=jnp.int32)

    def row_step(index, result):
        pick = (places == index).astype(jnp.float32)
        row_here = jnp.dot(pick, lower, precision=high)
        pivot = jnp.dot(row_here, pick, precision=high)
        before = jnp.where(places < index, row_here, 0.0)
        fresh = (pick - jnp.dot(before, result, precision=high)) / pivot
        return result + pick[:, None] * fresh[None, :]

    return lax.fori_loop(0, width, row_step, jnp.zeros_like(lower))


def gram_inverse(gram):
    high = lax.Precision.HIGHEST
    blocks = 4
    width = gram.shape[0] // blocks

    def piece(matrix, first, second):
        return matrix[first * width : (first + 1) * width, second * width : (second + 1) * width]

    lower = {}
    diag_inv = {}
    for col in range(blocks):
        square = piece(gram, col, col)
        for inner in range(col):
            square = square - jnp.dot(lower[col, inner], lower[col, inner].T, precision=high)
        lower[col, col] = small_factor(square)
        diag_inv[col] = small_inverse(lower[col, col])
        for below in range(col + 1, blocks):
            panel = piece(gram, below, col)
            for inner in range(col):
                panel = panel - jnp.dot(lower[below, inner], lower[col, inner].T, precision=high)
            lower[below, col] = jnp.dot(panel, diag_inv[col].T, precision=high)
    inv_blocks = {}
    for upper_row in range(blocks):
        inv_blocks[upper_row, upper_row] = diag_inv[upper_row]
        for col in range(upper_row - 1, -1, -1):
            total = jnp.zeros((width, width), jnp.float32)
            for inner in range(col, upper_row):
                total = total + jnp.dot(
                    lower[upper_row, inner], inv_blocks[inner, col], precision=high
                )
            inv_blocks[upper_row, col] = -jnp.dot(diag_inv[upper_row], total, precision=high)
    zero_block = jnp.zeros((width, width), jnp.float32)
    rows_list = []
    for upper_row in range(blocks):
        rows_list.append(
            jnp.concatenate(
                [
                    inv_blocks[upper_row, col] if col <= upper_row else zero_block
                    for col in range(blocks)
                ],
                axis=1,
            )
        )
    factor_inv = jnp.concatenate(rows_list, axis=0)
    return jnp.dot(factor_inv.T, factor_inv, precision=high, preferred_element_type=jnp.float32)


def shards(snapshots, modes, ridge):
    high = lax.Precision.HIGHEST
    nodes_total = modes.shape[0] * lax.axis_size("row")
    regrouped = lax.all_to_all(snapshots, "tm", split_axis=0, concat_axis=1, tiled=True)
    count = regrouped.shape[0]
    times_total = regrouped.shape[1]
    sub_modes = lax.dynamic_slice_in_dim(modes, lax.axis_index("tm") * count, count, 0)
    partial_sum = jnp.dot(
        sub_modes.T, regrouped, precision=high, preferred_element_type=jnp.float32
    )
    summed = lax.psum(partial_sum, ("row", "tm"))
    coords = summed / nodes_total
    feats = quad_features(coords)
    resid = regrouped - jnp.dot(
        sub_modes, coords, precision=high, preferred_element_type=jnp.float32
    )
    gram = jnp.dot(
        feats, feats.T, precision=high, preferred_element_type=jnp.float32
    ) + times_total * jnp.diag(ridge)
    inverse = gram_inverse(gram)
    cross = lax.dot_general(
        resid, feats, (((1,), (1,)), ((), ())), precision=high, preferred_element_type=jnp.float32
    )
    return jnp.dot(cross, inverse, precision=high, preferred_element_type=jnp.float32)


def solution(mesh):
    return jax.shard_map(
        shards,
        mesh=mesh,
        in_specs=(P("row", "tm"), P("row", None), P()),
        out_specs=P(("row", "tm"), None),
        check_vma=False,
    )
```

profile of v0, /device:TPU:1, one launch (start us, length us, event | category | flops | bytes accessed | tf_op | source)
XLA Modules:
  0.0 2371.8 jit_solution(17554813717827526186)
XLA Ops:
  6.5 5.0 all-to-all-start
  11.6 46.7 %all-to-all-done = f32[4,2048,128]{2,1,0:T(8,128)} async-done(((f32[4,2048,128]{2,1,0:T(8,128)}), f32[4,2048,128]{2,1,0:T(8,128)}, u32[]{:S(2)}, u32[]{:S(2)}) %all-to-all-start) | async-done | bytes 4194336 | tf_op jit(solution)/shard_map/all_to_all | solution.py:97
  58.4 5.3 copy.8
  63.7 6.7 fusion.112
  70.5 5.4 copy.9
  75.9 236.8 %all-reduce.3.cloned.1.call-done = f32[32,512]{1,0:T(8,128)} async-done(((f32[32,512]{1,0:T(8,128)}), f32[32,512]{1,0:T(8,128)}) %all-reduce.3.cloned.1.call-update) | async-done | bytes 65552 | tf_op jit(solution)/shard_map/psum | solution.py:104
  313.5 2.2 gather_fusion
  315.7 2.9 gather_fusion.1
  318.6 4.4 convolution_add_fusion
  324.1 275.1 %while.120 = (s32[]{:T(128)}, f32[132,132]{1,0:T(8,128)S(1)}, f32[132,132]{1,0:T(8,128)S(1)}, s32[]{:T(128)}, s32[]{:T(128)}) while((s32[]{:T(128)}, f32[132,132]{1,0:T(8,128)S(1)}, f32[132,132]{1,0:T(8,128)S(1)}, s32[]{:T(128)}, s32[]{:T(128)}) %tuple.293), condition=%wide.region_2.3_spmd.clone.clone, body=%wide.region_1.2_spmd.clone.clone.sunk | while | flops 715574 | bytes 355585 | solution.py:28
  599.2 219.0 %while.121 = (s32[]{:T(128)}, f32[132,132]{1,0:T(8,128)S(1)}, f32[132,132]{1,0:T(8,128)S(1)}, s32[]{:T(128)}, s32[]{:T(128)}) while((s32[]{:T(128)}, f32[132,132]{1,0:T(8,128)S(1)}, f32[132,132]{1,0:T(8,128)S(1)}, s32[]{:T(128)}, s32[]{:T(128)}) %tuple.296), condition=%wide.region_4.5_spmd.clone.clone, body=%wide.region_3.4_spmd.clone.clone.sunk | while | flops 489326 | bytes 284692 | solution.py:44
  818.2 1.3 fusion.114
  820.7 1.9 convolution_subtract_fusion.5
  828.5 287.1 %while.122 = (s32[]{:T(128)}, f32[132,132]{1,0:T(8,128)S(1)}, f32[132,132]{1,0:T(8,128)S(1)}, s32[]{:T(128)}, s32[]{:T(128)}) while((s32[]{:T(128)}, f32[132,132]{1,0:T(8,128)S(1)}, f32[132,132]{1,0:T(8,128)S(1)}, s32[]{:T(128)}, s32[]{:T(128)}) %tuple.299), condition=%wide.region_6.7_spmd.clone.clone, body=%wide.region_5.6_spmd.clone.clone.sunk | while | flops 715574 | bytes 355585 | solution.py:28
  1115.6 229.7 %while.123 = (s32[]{:T(128)}, f32[132,132]{1,0:T(8,128)S(1)}, f32[132,132]{1,0:T(8,128)S(1)}, s32[]{:T(128)}, s32[]{:T(128)}) while((s32[]{:T(128)}, f32[132,132]{1,0:T(8,128)S(1)}, f32[132,132]{1,0:T(8,128)S(1)}, s32[]{:T(128)}, s32[]{:T(128)}) %tuple.302), condition=%wide.region_8.9_spmd.clone.clone, body=%wide.region_7.8_spmd.clone.clone.sunk | while | flops 489326 | bytes 284692 | solution.py:44
  1345.3 1.2 fusion.137
  1350.9 258.4 %while.124 = (s32[]{:T(128)}, f32[132,132]{1,0:T(8,128)S(1)}, f32[132,132]{1,0:T(8,128)S(1)}, s32[]{:T(128)}, s32[]{:T(128)}) while((s32[]{:T(128)}, f32[132,132]{1,0:T(8,128)S(1)}, f32[132,132]{1,0:T(8,128)S(1)}, s32[]{:T(128)}, s32[]{:T(128)}) %tuple.305), condition=%wide.region_10.11_spmd.clone.clone, body=%wide.region_9.10_spmd.clone.clone.sunk | while | flops 715574 | bytes 355585 | solution.py:28
  1609.3 217.9 %while.125 = (s32[]{:T(128)}, f32[132,132]{1,0:T(8,128)S(1)}, f32[132,132]{1,0:T(8,128)S(1)}, s32[]{:T(128)}, s32[]{:T(128)}) while((s32[]{:T(128)}, f32[132,132]{1,0:T(8,128)S(1)}, f32[132,132]{1,0:T(8,128)S(1)}, s32[]{:T(128)}, s32[]{:T(128)}) %tuple.308), condition=%wide.region_12.13_spmd.clone.clone, body=%wide.region_11.12_spmd.clone.clone.sunk | while | flops 489326 | bytes 284692 | solution.py:44
  1829.7 270.9 %while.126 = (s32[]{:T(128)}, f32[132,132]{1,0:T(8,128)S(1)}, f32[132,132]{1,0:T(8,128)S(1)}, s32[]{:T(128)}, s32[]{:T(128)}) while((s32[]{:T(128)}, f32[132,132]{1,0:T(8,128)S(1)}, f32[132,132]{1,0:T(8,128)S(1)}, s32[]{:T(128)}, s32[]{:T(128)}) %tuple.311), condition=%wide.region_14.15_spmd.clone.clone, body=%wide.region_13.14_spmd.clone.clone.sunk | while | flops 715574 | bytes 355585 | solution.py:28
  2100.7 230.4 %while.127 = (s32[]{:T(128)}, f32[132,132]{1,0:T(8,128)S(1)}, f32[132,132]{1,0:T(8,128)S(1)}, s32[]{:T(128)}, s32[]{:T(128)}) while((s32[]{:T(128)}, f32[132,132]{1,0:T(8,128)S(1)}, f32[132,132]{1,0:T(8,128)S(1)}, s32[]{:T(128)}, s32[]{:T(128)}) %tuple.314), condition=%wide.region_16.17_spmd.clone.clone, body=%wide.region_15.16_spmd.clone.clone.sunk | while | flops 489326 | bytes 284692 | solution.py:44
  2336.6 3.5 fusion.110
  2340.1 7.4 fusion.80
  2347.6 4.9 fusion.84
  2352.5 12.0 fusion.142
  (7995 shorter events, 1595.9 us)
Async XLA Ops:
  6.5 57.2 %copy-start = (f32[8192,32]{0,1:T(8,128)S(1)}, f32[8192,32]{0,1:T(8,128)}, u32[]{:S(2)}) copy-start(f32[8192,32]{0,1:T(8,128)} %param.24) | copy-start | bytes 3145732
  6.5 5.1 copy-start.14
  6.5 51.8 %all-to-all-start = ((f32[4,2048,128]{2,1,0:T(8,128)}), f32[4,2048,128]{2,1,0:T(8,128)}, u32[]{:S(2)}, u32[]{:S(2)}) async-start(f32[4,2048,128]{2,1,0:T(8,128)} %bitcast.233), calls=%async_computation | async-start | bytes 8388608 | tf_op jit(solution)/shard_map/all_to_all | solution.py:97
  11.5 301.2 %all-reduce.3.cloned.1.call-start = ((), (), s32[]{:S(2)}) async-start(), calls=%async_computation.1 | async-start | bytes 131072 | tf_op jit(solution)/shard_map/psum | solution.py:104
  63.7 6.7 copy-start.13
  315.7 2.9 copy-start.12
  323.0 1.1 copy-start.3
  818.2 4.4 copy-start.4
  1115.6 231.9 %copy-start.8 = (f32[132,132]{1,0:T(8,128)S(1)}, f32[132,132]{1,0:T(8,128)}, u32[]{:S(2)}) copy-start(f32[132,132]{1,0:T(8,128)} %convolution_subtract_fusion.5) | copy-start | bytes 209092
  1345.3 3.1 copy-start.9
  1345.3 5.3 copy-start.7
  1609.3 218.0 %copy-start.10 = (f32[132,132]{1,0:T(8,128)S(1)}, f32[132,132]{1,0:T(8,128)}, u32[]{:S(2)}) copy-start(f32[132,132]{1,0:T(8,128)} %convolution_subtract_fusion.1) | copy-start | bytes 209092
  2331.0 3.9 copy-start.6
  2331.0 4.4 copy-start.5
  2335.2 1.4 copy-start.11
  2336.0 4.1 copy-start.2
  2336.6 3.5 copy-start.1
Sparse Core Ops, SparseCore 0:
  70.5 242.1 all-reduce.2
where the time goes:
time: 2390 us; the launch traced here: 2370 us
  other arithmetic  1110 us (46%)
  matrix products  521 us (22%)
  loops' own time  414 us (17%)
  waiting for transfers between devices  284 us (12%)
  local copies, waits for them, and re-layouts  24.2 us (1%)
    another operation x4, loops' own time, small_factor(): return lax.fori_loop(0, width, column_step, jnp.zeros_like(block))  380 us
    dot_general x528, other arithmetic, column_step(): pivot = jnp.sqrt(jnp.dot(column, pick, precision=high))  362 us
    dot_general x528, other arithmetic, row_step(): pivot = jnp.dot(row_here, pick, precision=high)  320 us
    div x528, other arithmetic, row_step(): fresh = (pick - jnp.dot(before, result, precision=high)) / pivot  319 us
    psum x1, waiting for transfers between devices, shards(): summed = lax.psum(partial_sum, ('row', 'tm'))  237 us
    dot_general x528, matrix products, column_step(): row_here = jnp.dot(pick, lower, precision=high)  104 us
    dot_general x528, matrix products, column_step(): jnp.dot(lower, row_here, precision=high)  102 us
    dot_general x528, matrix products, column_step(): jnp.dot(block, pick, precision=high)  85 us

commit v1 on v0

v1 whole, which is shorter than its diff:
```python
import functools

import jax
import jax.numpy as jnp
import numpy as np
from jax import lax
from jax.experimental import pallas as pl
from jax.experimental.pallas import tpu as pltpu
from jax.sharding import PartitionSpec as P

R = 32
FEAT = R * (R + 1) // 2
F32 = jnp.float32
BF16 = jnp.bfloat16
LOW_LIMIT = 128.0
LOW_STOP = 0.05
FINE_STOP = 1e-3
FINE_MAX = 12


def split2(x):
    hi = x.astype(BF16)
    return hi, (x - hi.astype(F32)).astype(BF16)


def split3(x):
    hi = x.astype(BF16)
    rest = x - hi.astype(F32)
    mid = rest.astype(BF16)
    return hi, mid, (rest - mid.astype(F32)).astype(BF16)


def dot(a, b, dims=((1,), (0,))):
    return lax.dot_general(a, b, (dims, ((), ())), preferred_element_type=F32)


def dot3(a, b, dims=((1,), (0,))):
    ah, al = a
    bh, bl = b
    return dot(al, bh, dims) + dot(ah, bl, dims) + dot(ah, bh, dims)


def dot6(a, b, dims=((1,), (0,))):
    ah, am, al = a
    bh, bm, bl = b
    small = dot(al, bh, dims) + dot(ah, bl, dims) + dot(am, bm, dims)
    return small + (dot(am, bh, dims) + dot(ah, bm, dims)) + dot(ah, bh, dims)


def weights_kernel(coords_ref, scale_ref, wh_ref, wl_ref, packed_ref, feats, hmat, xmat):
    times = hmat.shape[0]
    coords = jnp.concatenate([coords_ref[c] for c in range(coords_ref.shape[0])], axis=1)
    ch, cm, cl = split3(coords)
    packed_ref[...] = jnp.concatenate([ch, cm, cl, ch, cm, ch], axis=0)
    start = 0
    for i in range(R):
        feats[start : start + R - i, :] = (
            coords[i : i + 1, :] * coords[i:, :] * scale_ref[start : start + R - i, :]
        )
        start += R - i
    scaled = feats[...]
    eye = (
        lax.broadcasted_iota(jnp.int32, (times, times), 0)
        == lax.broadcasted_iota(jnp.int32, (times, times), 1)
    ).astype(F32)
    hmat[...] = eye + dot6(split3(scaled.T), split3(scaled))
    upper = jnp.max(jnp.sum(jnp.abs(hmat[...]), axis=0, keepdims=True))
    first = 2.0 / (1.0 + upper)
    rho = (upper - 1.0) * first * 0.5
    gain = 2.0 / (2.0 - rho * rho)
    xmat[...] = (gain * first) * (2.0 * eye - first * hmat[...])
    rho = rho * rho * 0.5 * gain

    def low_step(rho):
        gain = 2.0 / (2.0 - rho * rho)
        x = xmat[...].astype(BF16)
        turn = 2.0 * eye - dot(hmat[...].astype(BF16), x)
        xmat[...] = gain * dot(x, turn.astype(BF16))
        return rho * rho * 0.5 * gain

    def high_step(rho):
        gain = 2.0 / (2.0 - rho * rho)
        x = split3(xmat[...])
        turn = 2.0 * eye - dot6(split3(hmat[...]), x)
        xmat[...] = gain * dot6(x, split3(turn))
        return rho * rho * 0.5 * gain

    easy = upper <= LOW_LIMIT
    rho = lax.while_loop(lambda r: jnp.logical_and(easy, r > LOW_STOP), low_step, rho)
    rho = lax.while_loop(lambda r: r > LOW_STOP, high_step, rho)

    def fine_step(state):
        step, _ = state
        x = xmat[...]
        rest = eye - dot6(split3(hmat[...]), split3(x))
        size = jnp.max(jnp.sum(jnp.abs(rest), axis=0, keepdims=True))
        xmat[...] = x + dot3(split2(x), split2(rest))
        return step + 1, size

    lax.while_loop(
        lambda s: jnp.logical_and(s[0] < FINE_MAX, s[1] > FINE_STOP),
        fine_step,
        (jnp.int32(0), jnp.float32(1.0)),
    )
    w = dot6(split3(feats[...]), split3(xmat[...])) * scale_ref[...]
    wh, wl = split2(w)
    wh_ref[...] = wh
    wl_ref[...] = wl


def weights(coords, ridge):
    times = coords.shape[0] * coords.shape[2]
    root = lax.rsqrt(ridge * times)
    vmem = pl.BlockSpec(memory_space=pltpu.VMEM)
    return pl.pallas_call(
        weights_kernel,
        out_shape=[jax.ShapeDtypeStruct((FEAT, times), BF16)] * 2
        + [jax.ShapeDtypeStruct((6 * R, times), BF16)],
        in_specs=[vmem] * 2,
        out_specs=[vmem] * 3,
        scratch_shapes=[
            pltpu.VMEM((FEAT, times), F32),
            pltpu.VMEM((times, times), F32),
            pltpu.VMEM((times, times), F32),
        ],
        compiler_params=pltpu.CompilerParams(vmem_limit_bytes=48 * 2**20),
        cost_estimate=pl.CostEstimate(
            flops=2 * times**3 * 60, bytes_accessed=4 * times * FEAT, transcendentals=0
        ),
    )(coords, root[:, None])


def correction_kernel(blocks_ref, modes_ref, coords_ref, wh_ref, wl_ref, out_ref):
    snaps = jnp.concatenate([blocks_ref[b] for b in range(blocks_ref.shape[0])], axis=1)
    resid = snaps - dot(modes_ref[...], coords_ref[...])
    rh, rl = split2(resid)
    last = ((1,), (1,))
    wh = wh_ref[...]
    out_ref[...] = dot(wh, rl, last) + dot(wl_ref[...], rh, last) + dot(wh, rh, last)


def exact_split3(x):
    hi = lax.reduce_precision(x, 8, 7)
    mid = lax.reduce_precision(x - hi, 8, 7)
    low = x - hi - mid
    return hi.astype(BF16), mid.astype(BF16), low.astype(BF16)


def correct(blocks, modes6, coords6, wh, wl, tile=512):
    parts, count, width = blocks.shape
    times = parts * width
    depth = modes6.shape[1]
    return pl.pallas_call(
        correction_kernel,
        grid=(count // tile,),
        out_shape=jax.ShapeDtypeStruct((FEAT, count), F32),
        in_specs=[
            pl.BlockSpec((parts, tile, width), lambda i: (0, i, 0)),
            pl.BlockSpec((tile, depth), lambda i: (i, 0)),
            pl.BlockSpec((depth, times), lambda i: (0, 0)),
            pl.BlockSpec((FEAT, times), lambda i: (0, 0)),
            pl.BlockSpec((FEAT, times), lambda i: (0, 0)),
        ],
        out_specs=pl.BlockSpec((FEAT, tile), lambda i: (0, i)),
        compiler_params=pltpu.CompilerParams(vmem_limit_bytes=32 * 2**20),
        cost_estimate=pl.CostEstimate(
            flops=2 * count * times * FEAT * 3, bytes_accessed=12 * 2**20, transcendentals=0
        ),
    )(blocks, modes6, coords6, wh, wl)


GROUP = 8
MESH = pl.DeviceIdType.MESH


def project_kernel(modes_ref, snaps_ref, out_ref):
    @pl.when(pl.program_id(0) == 0)
    def _():
        out_ref[...] = jnp.zeros_like(out_ref)

    both = jnp.concatenate(split2(modes_ref[...]), axis=0)
    sh, sl = split2(snaps_ref[...])
    found = dot(both, sl) + dot(both, sh)
    out_ref[...] += found[R:] + found[:R]


def project(modes_t, snaps, step=2048):
    nodes, width = snaps.shape
    return pl.pallas_call(
        project_kernel,
        grid=(nodes // step,),
        out_shape=jax.ShapeDtypeStruct((R, width), F32),
        in_specs=[
            pl.BlockSpec((R, step), lambda i: (0, i)),
            pl.BlockSpec((step, width), lambda i: (i, 0)),
        ],
        out_specs=pl.BlockSpec((R, width), lambda i: (0, 0)),
        compiler_params=pltpu.CompilerParams(vmem_limit_bytes=32 * 2**20),
        cost_estimate=pl.CostEstimate(
            flops=6 * nodes * R * width, bytes_accessed=5 * 2**20, transcendentals=0
        ),
    )(modes_t, snaps)


def coords_kernel(scale, *refs):
    cols = len(refs) - 11
    parts, out_ref = refs[:cols], refs[cols]
    part, near, far, whole = refs[cols + 1 : cols + 5]
    near_send, near_recv, far_send, far_recv, whole_send, whole_recv = refs[cols + 5 :]
    row, col = lax.axis_index("row"), lax.axis_index("tm")
    planes = far.shape[0]
    plane, spot = row // GROUP, row % GROUP

    def near_peer(k):
        return {"row": plane * GROUP + (spot + k) % GROUP}

    def far_peer(k):
        return {"row": ((plane + k) % planes) * GROUP + spot}

    barrier = pltpu.get_barrier_semaphore()

    def greet(peer):
        pl.semaphore_signal(barrier, inc=1, device_id=peer, device_id_type=MESH)

    lax.fori_loop(1, GROUP, lambda k, _: greet(near_peer(k)), None)
    lax.fori_loop(1, planes, lambda k, _: greet(far_peer(k)), None)
    for c in range(cols):
        for s in range(GROUP):
            part[s, c] = parts[c][4 * s : 4 * s + 4, :]
    pl.semaphore_wait(barrier, GROUP - 1 + planes - 1)

    def near_copy(k):
        return pltpu.make_async_remote_copy(
            src_ref=part.at[(spot + k) % GROUP], dst_ref=near.at[spot],
            send_sem=near_send.at[k], recv_sem=near_recv.at[k],
            device_id=near_peer(k), device_id_type=MESH,
        )

    def far_copy(k):
        return pltpu.make_async_remote_copy(
            src_ref=far.at[plane], dst_ref=far.at[plane],
            send_sem=far_send.at[k], recv_sem=far_recv.at[k],
            device_id=far_peer(k), device_id_type=MESH,
        )

    def whole_copy(k):
        return pltpu.make_async_remote_copy(
            src_ref=whole.at[spot], dst_ref=whole.at[spot],
            send_sem=whole_send.at[k], recv_sem=whole_recv.at[k],
            device_id=near_peer(k), device_id_type=MESH,
        )

    lax.fori_loop(1, GROUP, lambda k, _: near_copy(k).start(), None)
    near[spot] = part[spot]
    lax.fori_loop(1, GROUP, lambda k, _: near_copy(k).wait_recv(), None)
    far[plane] = jnp.sum(near[...], axis=0)
    lax.fori_loop(1, planes, lambda k, _: far_copy(k).start(), None)
    lax.fori_loop(1, GROUP, lambda k, _: near_copy(k).wait_send(), None)
    lax.fori_loop(1, planes, lambda k, _: far_copy(k).wait_recv(), None)
    whole[spot] = jnp.sum(far[...], axis=0) * scale
    lax.fori_loop(1, GROUP, lambda k, _: whole_copy(k).start(), None)
    lax.fori_loop(1, planes, lambda k, _: far_copy(k).wait_send(), None)
    lax.fori_loop(1, GROUP, lambda k, _: whole_copy(k).wait(), None)
    for c in range(cols):
        place = (col + cols - c) % cols
        for s in range(GROUP):
            out_ref[place, 4 * s : 4 * s + 4, :] = whole[s, c]


def all_coords(parts, nodes_total):
    cols = len(parts)
    planes = lax.axis_size("row") // GROUP
    rows, width = parts[0].shape
    piece = (cols, rows // GROUP, width)
    dma = pltpu.SemaphoreType.DMA
    vmem = pl.BlockSpec(memory_space=pltpu.VMEM)
    return pl.pallas_call(
        functools.partial(coords_kernel, 1.0 / nodes_total),
        out_shape=jax.ShapeDtypeStruct((cols, rows, width), F32),
        in_specs=[vmem] * cols,
        out_specs=vmem,
        scratch_shapes=[
            pltpu.VMEM((GROUP,) + piece, F32),
            pltpu.VMEM((GROUP,) + piece, F32),
            pltpu.VMEM((planes,) + piece, F32),
            pltpu.VMEM((GROUP,) + piece, F32),
            dma((GROUP,)), dma((GROUP,)),
            dma((planes,)), dma((planes,)),
            dma((GROUP,)), dma((GROUP,)),
        ],
        compiler_params=pltpu.CompilerParams(collective_id=0, has_side_effects=True),
        cost_estimate=pl.CostEstimate(flops=10**6, bytes_accessed=2**20, transcendentals=0),
    )(*parts)


def shards(snapshots, modes, ridge):
    nodes_total = modes.shape[0] * lax.axis_size("row")
    parts = lax.axis_size("tm")
    count = snapshots.shape[0] // parts
    pieces = snapshots.reshape(parts, count, -1)
    mine = project(modes.T, snapshots)
    gathered = [mine] + [
        lax.ppermute(mine, "tm", [(i, (i + k) % parts) for i in range(parts)])
        for k in range(1, parts)
    ]
    gathered, pieces = lax.optimization_barrier((gathered, pieces))
    blocks = lax.all_to_all(pieces, "tm", split_axis=0, concat_axis=0, tiled=False)
    coords = all_coords(gathered, nodes_total)
    wh, wl, coords6 = weights(coords, ridge)
    sub = lax.dynamic_slice_in_dim(modes, lax.axis_index("tm") * count, count, 0)
    sub, _ = lax.optimization_barrier((sub, mine))
    mh, mm, ml = exact_split3(sub)
    modes6 = jnp.concatenate([mh, mh, mh, mm, mm, ml], axis=1)
    return correct(blocks, modes6, coords6, wh, wl).T


def solution(mesh):
    return jax.shard_map(
        shards,
        mesh=mesh,
        in_specs=(P("row", "tm"), P("row", None), P()),
        out_specs=P(("row", "tm"), None),
        check_vma=False,
    )
```

time: 2390 us -> 86.4 us (0.04)
  other arithmetic: 1110 us -> 0.28 us
  matrix products: 521 us -> 0 us
  loops' own time: 414 us -> 0 us
  waiting for transfers between devices: 284 us -> 3.19 us
  Pallas kernels: 0 us -> 65.4 us
    dot_general x1056 -> x0, other arithmetic: 683 us -> none  [the longest x528 362 us: column_step(): pivot = jnp.sqrt(jnp.dot(column, pick, precision=high))]
    dot_general x2678 -> x0, matrix products: 521 us -> none  [the longest x528 104 us: column_step(): row_here = jnp.dot(pick, lower, precision=high)]
    another operation x8 -> x0, loops' own time: 414 us -> none  [the longest x4 380 us: small_factor(): return lax.fori_loop(0, width, column_step, jnp.zeros_like(block))]
    div x529 -> x0, other arithmetic: 320 us -> none  [the longest x528 319 us: row_step(): fresh = (pick - jnp.dot(before, result, precision=high)) / pivot]
    psum x1 -> x0, waiting for transfers between devices: 237 us -> none  [shards(): summed = lax.psum(partial_sum, ('row', 'tm'))]
    add x1056 -> x0, other arithmetic: 98.2 us -> none  [the longest x528 49.1 us: column_step(): return lower + scaled[:, None] * pick[None, :]]
    pallas_call x0 -> x4, Pallas kernels: none -> 65.4 us  [the longest x1 32.9 us: weights(): pl.pallas_call(weights_kernel, out_shape=[jax.ShapeDtypeStruct((FEAT, tim...]
    all_to_all x1, waiting for transfers between devices: 46.7 us -> 0.01 us  [shards(): lax.all_to_all(pieces, 'tm', split_axis=0, concat_axis=0, tiled=False)]
where the time goes in v1:
time: 86.4 us; the launch traced here: 86 us
  Pallas kernels  65.4 us (76%)
  starting transfers between devices  9.36 us (11%)
  local copies, waits for them, and re-layouts  7.55 us (9%)
  waiting for transfers between devices  3.19 us (4%)
    pallas_call x1, Pallas kernels, weights(): pl.pallas_call(weights_kernel, out_shape=[jax.ShapeDtypeStruct((FEAT, tim...  32.9 us
    pallas_call x1, Pallas kernels, all_coords(): pl.pallas_call(functools.partial(coords_kernel, 1.0 / nodes_total), out_s...  23.4 us
    pallas_call x1, Pallas kernels, correct(): pl.pallas_call(correction_kernel, grid=(count // tile,), out_shape=jax.Sh...  7.69 us
    all_to_all x1, starting transfers between devices, shards(): lax.all_to_all(pieces, 'tm', split_axis=0, concat_axis=0, tiled=False)  4.85 us
    unnamed x16, local copies, waits for them, and re-layouts  4.85 us
    ppermute x3, starting transfers between devices, shards(): lax.ppermute(mine, 'tm', [(i, (i + k) % parts) for i in range(parts)])  4.51 us
    ppermute x3, waiting for transfers between devices, shards(): lax.ppermute(mine, 'tm', [(i, (i + k) % parts) for i in range(parts)])  3.19 us
  transfers between devices with their start and end apart: 4, of which 2 were waited for; matrix products, arithmetic and copies ran while one was open for 3% of the time, Pallas kernels for 65%

profile of v1, /device:TPU:1, one launch (start us, length us, event | category | flops | bytes accessed | tf_op | source)
XLA Modules:
  0.0 86.0 jit_solution(12894467587200558768)
XLA Ops:
  0.0 2.2 %copy-done = f32[8192,128]{1,0:T(8,128)S(1)} copy-done((f32[8192,128]{1,0:T(8,128)S(1)}, f32[8192,128]{1,0:T(8,128)}, u32[]{:S(2)}) %copy-start) | copy-done | bytes 4194328
  2.2 1.2 %copy-done.1 = f32[8192,32]{0,1:T(8,128)S(1)} copy-done((f32[8192,32]{0,1:T(8,128)S(1)}, f32[8192,32]{0,1:T(8,128)}, u32[]{:S(2)}) %copy-start.1) | copy-done | bytes 1048600
  3.4 1.4 %shard_map.37.refs_0_ = f32[32,128]{1,0:T(8,128)S(1)} custom-call(f32[32,8192]{1,0:T(8,128)S(1)} %bitcast.4, f32[8192,128]{1,0:T(8,128)S(1)} %copy-done), custom_call_target="tpu_custom_call" | custom-call | flops 201326592 | bytes 5242880 | tf_op jit(solution)/shard_map/pallas_call | solution.py:189
  4.9 0.0 copy-start.2
  4.9 3.4 %collective-permute-start.2 = (f32[32,128]{1,0:T(8,128)S(1)}, f32[32,128]{1,0:T(8,128)S(1)}, u32[]{:S(2)}, u32[]{:S(2)}) collective-permute-start(f32[32,128]{1,0:T(8,128)S(1)} %shard_map.37.refs_0_), channel_id=1, source_target_pairs={{0,3},{1,0},{2,1},{3,2},{4,7},{5,4},{6,5},{7,6},{8,11},{9,8},{10,9... | collective-permute-start | bytes 49160 | tf_op jit(solution)/shard_map/ppermute | solution.py:303
  8.3 0.5 collective-permute-start.1
  8.8 0.6 collective-permute-start
  9.4 0.0 collective-permute-done.2.refs_3_
  9.4 3.0 %collective-permute-done.1.refs_2_ = f32[32,128]{1,0:T(8,128)S(1)} collective-permute-done((f32[32,128]{1,0:T(8,128)S(1)}, f32[32,128]{1,0:T(8,128)S(1)}, u32[]{:S(2)}, u32[]{:S(2)}) %collective-permute-start.1) | collective-permute-done | bytes 16416 | tf_op jit(solution)/shard_map/ppermute | solution.py:303
  12.4 0.2 collective-permute-done.refs_1_
  12.6 0.0 copy-done.2
  12.6 0.4 copy-done.5
  13.0 0.2 copy-done.6
  13.2 4.9 %all-to-all-start = ((f32[4,2048,128]{2,1,0:T(8,128)}), f32[4,2048,128]{2,1,0:T(8,128)}, u32[]{:S(2)}, u32[]{:S(2)}) async-start(f32[4,2048,128]{2,1,0:T(8,128)} %bitcast.3), calls=%async_computation | async-start | bytes 8388608 | tf_op jit(solution)/shard_map/all_to_all | solution.py:307
  18.1 0.1 broadcast_in_dim.4.scale_ref
  18.2 1.0 %constant_dynamic-slice_fusion = f32[2048,32]{0,1:T(8,128)S(1)} fusion(f32[8192,32]{0,1:T(8,128)} %param.4, s32[]{:T(128)S(6)} %select_n.3), kind=kLoop, calls=%fused_computation.6 | loop fusion | bytes 524292 | tf_op jit(solution)/shard_map/dynamic_slice | solution.py:310
  19.2 0.3 copy.7
  19.5 0.3 fusion
  19.8 1.3 %concatenate.3.modes_ref = bf16[2048,192]{1,0:T(8,128)(2,1)S(1)} concatenate(bf16[2048,32]{1,0:T(8,128)(2,1)S(1)} %get-tuple-element.25, bf16[2048,32]{1,0:T(8,128)(2,1)S(1)} %get-tuple-element.25, bf16[2048,32]{1,0:T(8,128)(2,1)S(1)} %get-tuple-element.25, bf16[2048,32]{1,0:T(8,128)(2,1)S(1)} %get-tuple-element.24, bf16[2048,32]{1,0:T(8,128)(2,1)S(1)} %get-tuple-element.24, ...), dimensions={1} | concatenate | bytes 1572864 | tf_op jit(solution)/shard_map/concatenate | solution.py:313
  21.1 23.4 %shard_map.38.coords_ref = f32[4,32,128]{2,1,0:T(8,128)} custom-call(f32[32,128]{1,0:T(8,128)} %copy-done.2, f32[32,128]{1,0:T(8,128)} %copy-done.6, f32[32,128]{1,0:T(8,128)} %copy-done.5, f32[32,128]{1,0:T(8,128)} %copy-done.4), custom_call_target="tpu_custom_call" | custom-call | flops 1000000 | bytes 1048576 | tf_op jit(solution)/shard_map/pallas_call | solution.py:277
  44.5 0.8 copy-done.3
  45.4 32.9 %shard_map.39 = (bf16[528,512]{1,0:T(8,128)(2,1)S(1)}, bf16[528,512]{1,0:T(8,128)(2,1)S(1)}, bf16[192,512]{1,0:T(8,128)(2,1)S(1)}) custom-call(f32[4,32,128]{2,1,0:T(8,128)S(1)} %copy-done.3, f32[528,1]{1,0:T(8,128)S(1)} %broadcast_in_dim.4.scale_ref), custom_call_target="tpu_custom_call" | custom-call | flops 16106127360 | bytes 1081344 | tf_op jit(solution)/shard_map/pallas_call | solution.py:115
  78.3 0.0 all-to-all-done.blocks_ref
  78.3 7.7 %shard_map.40 = f32[528,2048]{1,0:T(8,128)} custom-call(f32[4,2048,128]{2,1,0:T(8,128)} %all-to-all-done.blocks_ref, bf16[2048,192]{1,0:T(8,128)(2,1)S(1)} %concatenate.3.modes_ref, bf16[192,512]{1,0:T(8,128)(2,1)S(1)} %get-tuple-element.20.coords_ref, bf16[528,512]{1,0:T(8,128)(2,1)S(1)} %get-tuple-element.21.wh_ref, ...), custom_call_target="tpu_custom_call" | custom-call | flops 3321888768 | bytes 12582912 | tf_op jit(solution)/shard_map/pallas_call | solution.py:153
  (10 shorter events, 0.0 us)
Async XLA Ops:
  0.0 2.2 %copy-start = (f32[8192,128]{1,0:T(8,128)S(1)}, f32[8192,128]{1,0:T(8,128)}, u32[]{:S(2)}) copy-start(f32[8192,128]{1,0:T(8,128)} %snaps_ref.1) | copy-start | bytes 12582916
  2.2 1.2 %copy-start.1 = (f32[8192,32]{0,1:T(8,128)S(1)}, f32[8192,32]{0,1:T(8,128)}, u32[]{:S(2)}) copy-start(f32[8192,32]{0,1:T(8,128)} %param.4) | copy-start | bytes 3145732
  4.9 7.7 %copy-start.2 = (f32[32,128]{1,0:T(8,128)}, f32[32,128]{1,0:T(8,128)S(1)}, u32[]{:S(2)}) copy-start(f32[32,128]{1,0:T(8,128)S(1)} %shard_map.37.refs_0_) | copy-start | bytes 49156
  4.9 4.5 %collective-permute-start.2 = (f32[32,128]{1,0:T(8,128)S(1)}, f32[32,128]{1,0:T(8,128)S(1)}, u32[]{:S(2)}, u32[]{:S(2)}) collective-permute-start(f32[32,128]{1,0:T(8,128)S(1)} %shard_map.37.refs_0_), channel_id=1, source_target_pairs={{0,3},{1,0},{2,1},{3,2},{4,7},{5,4},{6,5},{7,6},{8,11},{9,8},{10,9... | collective-permute-start | bytes 49160 | tf_op jit(solution)/shard_map/ppermute | solution.py:303
  8.3 4.1 %collective-permute-start.1 = (f32[32,128]{1,0:T(8,128)S(1)}, f32[32,128]{1,0:T(8,128)S(1)}, u32[]{:S(2)}, u32[]{:S(2)}) collective-permute-start(f32[32,128]{1,0:T(8,128)S(1)} %shard_map.37.refs_0_), channel_id=1, source_target_pairs={{0,2},{1,3},{2,0},{3,1},{4,6},{5,7},{6,4},{7,5},{8,10},{9,11},{10,... | collective-permute-start | bytes 49160 | tf_op jit(solution)/shard_map/ppermute | solution.py:303
  8.8 3.8 %collective-permute-start = (f32[32,128]{1,0:T(8,128)S(1)}, f32[32,128]{1,0:T(8,128)S(1)}, u32[]{:S(2)}, u32[]{:S(2)}) collective-permute-start(f32[32,128]{1,0:T(8,128)S(1)} %shard_map.37.refs_0_), channel_id=1, source_target_pairs={{0,1},{1,2},{2,3},{3,0},{4,5},{5,6},{6,7},{7,4},{8,9},{9,10},{10,1... | collective-permute-start | bytes 49160 | tf_op jit(solution)/shard_map/ppermute | solution.py:303
  9.4 3.2 %copy-start.4 = (f32[32,128]{1,0:T(8,128)}, f32[32,128]{1,0:T(8,128)S(1)}, u32[]{:S(2)}) copy-start(f32[32,128]{1,0:T(8,128)S(1)} %collective-permute-done.2.refs_3_) | copy-start | bytes 49156
  12.4 0.6 copy-start.5
  12.6 0.6 copy-start.6
  12.6 5.5 %copy-start.7 = (f32[528]{0:T(1024)S(1)}, f32[528]{0:T(1024)}, u32[]{:S(2)}) copy-start(f32[528]{0:T(1024)} %param.5) | copy-start | bytes 6340
  13.2 65.1 %all-to-all-start = ((f32[4,2048,128]{2,1,0:T(8,128)}), f32[4,2048,128]{2,1,0:T(8,128)}, u32[]{:S(2)}, u32[]{:S(2)}) async-start(f32[4,2048,128]{2,1,0:T(8,128)} %bitcast.3), calls=%async_computation | async-start | bytes 8388608 | tf_op jit(solution)/shard_map/all_to_all | solution.py:307
  44.5 0.8 copy-start.3

commit v2 on v0

v2 whole, which is shorter than its diff:
```python
import functools

import jax
import jax.numpy as jnp
import numpy as np
from jax import lax
from jax.experimental import pallas as pl
from jax.experimental.pallas import tpu as pltpu
from jax.sharding import PartitionSpec as P

R = 32
FEAT = R * (R + 1) // 2
F32 = jnp.float32
BF16 = jnp.bfloat16
COARSE_STEPS = 5
FINE_STEPS = 2
FINE_STOP = 4e-3
HIGH_STOP = 0.05
FINE_MAX = 12
GROUP = 8
TILE = 512
CHUNKS = ((0, 256), (256, 256), (512, 512), (1024, 512), (1536, 512))
EARLY_CHUNKS = 1
MESH = pl.DeviceIdType.MESH


def split2(x):
    hi = x.astype(BF16)
    return hi, (x - hi.astype(F32)).astype(BF16)


def split3(x):
    hi = x.astype(BF16)
    rest = x - hi.astype(F32)
    mid = rest.astype(BF16)
    return hi, mid, (rest - mid.astype(F32)).astype(BF16)


def dot(a, b, dims=((1,), (0,))):
    return lax.dot_general(a, b, (dims, ((), ())), preferred_element_type=F32)


def dot3(a, b, dims=((1,), (0,))):
    ah, al = a
    bh, bl = b
    return dot(al, bh, dims) + dot(ah, bl, dims) + dot(ah, bh, dims)


def dot6(a, b, dims=((1,), (0,))):
    ah, am, al = a
    bh, bm, bl = b
    small = dot(al, bh, dims) + dot(ah, bl, dims) + dot(am, bm, dims)
    return small + (dot(am, bh, dims) + dot(ah, bm, dims)) + dot(ah, bh, dims)


def identity(size):
    down = lax.broadcasted_iota(jnp.int32, (size, size), 0)
    return (down == lax.broadcasted_iota(jnp.int32, (size, size), 1)).astype(F32)


def column_scale(ridge_ref, times):
    row = lax.rsqrt(ridge_ref[...] * times)
    return jnp.sum(identity(FEAT) * row, axis=1, keepdims=True)


def pack6(parts):
    hi, mid, low = parts
    return jnp.concatenate([hi, mid, low, hi, mid, hi], axis=0)


def fill_feats(coords, scale, feats):
    start = 0
    for i in range(R):
        feats[start : start + R - i, :] = (
            coords[i : i + 1, :] * coords[i:, :] * scale[start : start + R - i, :]
        )
        start += R - i


def first_guess(feats, hmat, xmat):
    eye = identity(hmat.shape[0])
    scaled = feats[...]
    hmat[...] = eye + dot6(split3(scaled.T), split3(scaled))
    upper = jnp.max(jnp.sum(jnp.abs(hmat[...]), axis=0, keepdims=True), axis=1, keepdims=True)
    first = 2.0 / (1.0 + upper)
    rho = (upper - 1.0) * first * 0.5
    gain = 2.0 / (2.0 - rho * rho)
    xmat[...] = (gain * first) * (2.0 * eye - first * hmat[...])
    return rho * rho * 0.5 * gain


def coarse_step(hmat, xmat, rho):
    gain = 2.0 / (2.0 - rho * rho)
    x = xmat[...].astype(BF16)
    turn = 2.0 * identity(hmat.shape[0]) - dot(hmat[...].astype(BF16), x)
    xmat[...] = gain * dot(x, turn.astype(BF16))
    return rho * rho * 0.5 * gain


def high_step(hmat, xmat, rho):
    gain = 2.0 / (2.0 - rho * rho)
    x = split3(xmat[...])
    turn = 2.0 * identity(hmat.shape[0]) - dot6(split3(hmat[...]), x)
    xmat[...] = gain * dot6(x, split3(turn))
    return rho * rho * 0.5 * gain


def fine_step(hmat, xmat):
    x = xmat[...]
    rest = identity(hmat.shape[0]) - dot6(split3(hmat[...]), split3(x))
    xmat[...] = x + dot3(split2(x), split2(rest))
    return jnp.max(jnp.sum(jnp.abs(rest), axis=0, keepdims=True), axis=1, keepdims=True)


def store_weights(feats, xmat, scale, wh_ref, wl_ref):
    wh, wl = split2(dot6(split3(feats[...]), split3(xmat[...])) * scale)
    wh_ref[...] = wh
    wl_ref[...] = wl


def corrected(snaps, modes_t, packed, wh, wl):
    mh, mm, ml = split3(modes_t)
    modes6 = jnp.concatenate([mh, mh, mh, mm, mm, ml], axis=0)
    resid = snaps - dot(modes6, packed, ((0,), (0,)))
    rh, rl = split2(resid)
    last = ((1,), (1,))
    return dot(wh, rl, last) + dot(wl, rh, last) + dot(wh, rh, last)


def main_kernel(nodes_total, done_tiles, snaps_ref, modes_ref, ridge_ref, *refs):
    outs = 5 + (done_tiles > 0)
    blocks_ref, coords_ref, wh_ref, wl_ref, size_ref = refs[:5]
    out_ref = refs[5] if done_tiles else None
    (
        snaps, modes_t, cross, near, far, whole, feats, hmat, xmat, packed, tiles, result,
        load_sem, cross_send, cross_recv, near_send, near_recv, far_send, far_recv,
        whole_send, whole_recv, block_send, block_recv, tile_sem, result_sem,
    ) = refs[outs:]
    row, col = lax.axis_index("row"), lax.axis_index("tm")
    cols, planes = cross.shape[0], far.shape[0]
    plane, spot = row // GROUP, row % GROUP
    count = snaps.shape[0] // cols
    times = hmat.shape[0]

    def cross_peer(k):
        return {"tm": (col + k) % cols}

    def near_peer(k):
        return {"row": plane * GROUP + (spot + k) % GROUP}

    def far_peer(k):
        return {"row": ((plane + k) % planes) * GROUP + spot}

    def remote(src, dst, send, recv, peer):
        return pltpu.make_async_remote_copy(
            src_ref=src, dst_ref=dst, send_sem=send, recv_sem=recv,
            device_id=peer, device_id_type=MESH,
        )

    def block_copy(k, c):
        start, size = CHUNKS[c]
        source = snaps_ref.at[pl.ds(((col + k) % cols) * count + start, size), :]
        return remote(
            source, blocks_ref.at[k - 1, pl.ds(start, size), :],
            block_send.at[k, c], block_recv.at[k, c], cross_peer(k),
        )

    def cross_copy(k):
        return remote(cross.at[0], cross.at[k], cross_send.at[k], cross_recv.at[k], cross_peer(k))

    def near_copy(k):
        return remote(
            cross.at[:, (spot + k) % GROUP], near.at[spot],
            near_send.at[k], near_recv.at[k], near_peer(k),
        )

    def far_copy(k):
        return remote(far.at[plane], far.at[plane], far_send.at[k], far_recv.at[k], far_peer(k))

    def whole_copy(k):
        return remote(
            whole.at[spot], whole.at[spot], whole_send.at[k], whole_recv.at[k], near_peer(k)
        )

    def load(c):
        rows = pl.ds(c * count, count)
        return pltpu.make_async_copy(snaps_ref.at[rows, :], snaps.at[rows, :], load_sem.at[c])

    modes_load = pltpu.make_async_copy(modes_ref, modes_t, load_sem.at[cols])
    modes_load.start()
    for c in range(cols):
        load(c).start()
    barrier = pltpu.get_barrier_semaphore()
    peers = [cross_peer(k) for k in range(1, cols)]
    peers += [near_peer(k) for k in range(1, GROUP)] + [far_peer(k) for k in range(1, planes)]
    for peer in peers:
        pl.semaphore_signal(barrier, inc=1, device_id=peer, device_id_type=MESH)
    pl.semaphore_wait(barrier, len(peers))

    order = [1, cols - 1] + list(range(2, cols - 1))
    for c in range(EARLY_CHUNKS):
        for k in order:
            block_copy(k, c).start()

    modes_load.wait()
    total = jnp.zeros((2 * R, snaps.shape[1]), F32)
    for c in range(cols):
        load(c).wait()
        both = jnp.concatenate(split2(modes_t[:, c * count : (c + 1) * count]), axis=0)
        sh, sl = split2(snaps[c * count : (c + 1) * count, :])
        total += dot(both, sl) + dot(both, sh)
    mine = total[R:] + total[:R]
    share = R // GROUP
    for s in range(GROUP):
        cross[0, s] = mine[share * s : share * (s + 1), :]
    for k in order:
        cross_copy(k).start()
    for c in range(EARLY_CHUNKS, len(CHUNKS)):
        for k in order:
            block_copy(k, c).start()
    scale = column_scale(ridge_ref, times)
    for k in order:
        cross_copy(k).wait_recv()
    for k in range(1, GROUP):
        near_copy(k).start()
    near[spot] = cross[:, spot]
    for k in range(1, GROUP):
        near_copy(k).wait_recv()
    far[plane] = jnp.sum(near[...], axis=0)
    for k in range(1, planes):
        far_copy(k).start()
    for k in range(1, planes):
        far_copy(k).wait_recv()
    whole[spot] = jnp.sum(far[...], axis=0) * (1.0 / nodes_total)
    for k in range(1, GROUP):
        whole_copy(k).start()
    for k in range(1, GROUP):
        whole_copy(k).wait_recv()
    width = snaps.shape[1]
    for c in range(cols):
        for s in range(GROUP):
            coords_ref[share * s : share * (s + 1), c * width : (c + 1) * width] = whole[s, c]

    coords = coords_ref[...]
    packed[...] = pack6(split3(coords))
    fill_feats(coords, scale, feats)
    rho = first_guess(feats, hmat, xmat)
    rho = lax.fori_loop(0, COARSE_STEPS, lambda _, r: coarse_step(hmat, xmat, r), rho)
    size = lax.fori_loop(0, FINE_STEPS, lambda _, r: fine_step(hmat, xmat), rho)
    size_ref[...] = jnp.broadcast_to(size, size_ref.shape)
    store_weights(feats, xmat, scale, wh_ref, wl_ref)

    for t in range(len(CHUNKS)):
        start, size = CHUNKS[t]
        for k in order:
            block_copy(k, t).wait_recv()
        if start + size > done_tiles * TILE or (start + size) % TILE:
            continue
        tile = (start + size) // TILE - 1
        rows = pl.ds(tile * TILE, TILE)
        moves = [
            pltpu.make_async_copy(
                blocks_ref.at[k - 1, rows, :], tiles.at[k - 1], tile_sem.at[k]
            )
            for k in range(1, cols)
        ]
        for move in moves:
            move.start()
        for move in moves:
            move.wait()
        base = pl.multiple_of(col * count + tile * TILE, TILE)
        values = jnp.concatenate(
            [snaps[pl.ds(base, TILE), :]] + [tiles[k] for k in range(cols - 1)], axis=1
        )
        result[tile] = corrected(
            values, modes_t[:, pl.ds(base, TILE)], packed[...], wh_ref[...], wl_ref[...]
        )
        pltpu.make_async_copy(
            result.at[tile], out_ref.at[:, pl.ds(tile * TILE, TILE)], result_sem.at[tile]
        ).start()
    for tile in range(done_tiles):
        pltpu.make_async_copy(
            result.at[tile], out_ref.at[:, pl.ds(tile * TILE, TILE)], result_sem.at[tile]
        ).wait()
    for k in range(1, cols):
        cross_copy(k).wait_send()
        for c in range(len(CHUNKS)):
            block_copy(k, c).wait_send()
    for k in range(1, GROUP):
        near_copy(k).wait_send()
        whole_copy(k).wait_send()
    for k in range(1, planes):
        far_copy(k).wait_send()


def exchange_and_weigh(snapshots, modes_t, ridge, nodes_total, done_tiles):
    cols = lax.axis_size("tm")
    planes = lax.axis_size("row") // GROUP
    nodes, width = snapshots.shape
    count, times = nodes // cols, cols * width
    piece = (cols, R // GROUP, width)
    dma = pltpu.SemaphoreType.DMA
    vmem = pl.BlockSpec(memory_space=pltpu.VMEM)
    far_away = pl.BlockSpec(memory_space=pl.ANY)
    shape = jax.ShapeDtypeStruct
    out_shape = [
        shape((cols - 1, count, width), F32),
        shape((R, times), F32),
        shape((FEAT, times), BF16),
        shape((FEAT, times), BF16),
        shape((8, 128), F32),
    ]
    out_specs = [far_away, vmem, vmem, vmem, vmem]
    if done_tiles:
        out_shape.append(shape((FEAT, done_tiles * TILE), F32))
        out_specs.append(far_away)
    return pl.pallas_call(
        functools.partial(main_kernel, nodes_total, done_tiles),
        out_shape=out_shape,
        in_specs=[far_away, far_away, vmem],
        out_specs=out_specs,
        scratch_shapes=[
            pltpu.VMEM((nodes, width), F32),
            pltpu.VMEM((R, nodes), F32),
            pltpu.VMEM((cols, GROUP, R // GROUP, width), F32),
            pltpu.VMEM((GROUP,) + piece, F32),
            pltpu.VMEM((planes,) + piece, F32),
            pltpu.VMEM((GROUP,) + piece, F32),
            pltpu.VMEM((FEAT, times), F32),
            pltpu.VMEM((times, times), F32),
            pltpu.VMEM((times, times), F32),
            pltpu.VMEM((6 * R, times), BF16),
            pltpu.VMEM((cols - 1, TILE, width), F32),
            pltpu.VMEM((max(done_tiles, 1), FEAT, TILE), F32),
            dma((cols + 1,)),
            dma((cols,)), dma((cols,)),
            dma((GROUP,)), dma((GROUP,)),
            dma((planes,)), dma((planes,)),
            dma((GROUP,)), dma((GROUP,)),
            dma((cols, len(CHUNKS))), dma((cols, len(CHUNKS))),
            dma((cols,)),
            dma((max(done_tiles, 1),)),
        ],
        compiler_params=pltpu.CompilerParams(
            collective_id=0, has_side_effects=True, vmem_limit_bytes=44 * 2**20
        ),
        cost_estimate=pl.CostEstimate(flops=10**10, bytes_accessed=2**24, transcendentals=0),
    )(snapshots, modes_t, ridge.reshape(1, -1))


def final_kernel(done_tiles, place_ref, *refs):
    if done_tiles:
        done_ref, refs = refs[0], refs[1:]
    own_ref, blocks_ref, modes_ref, coords_ref, wh_ref, wl_ref, size_ref, ridge_ref = refs[:8]
    out_ref, wh_slow, wl_slow, feats, hmat, xmat, flag = refs[8:]
    step = pl.program_id(0)
    times = hmat.shape[0]

    @pl.when(step == 0)
    def _():
        good = jnp.max(size_ref[...]) <= FINE_STOP
        flag[0] = good.astype(jnp.int32)

        @pl.when(jnp.logical_not(good))
        def _():
            scale = column_scale(ridge_ref, times)
            fill_feats(coords_ref[...], scale, feats)
            rho = jnp.max(first_guess(feats, hmat, xmat))
            lax.while_loop(
                lambda r: r > HIGH_STOP, lambda r: high_step(hmat, xmat, r), rho
            )

            lax.while_loop(
                lambda s: jnp.logical_and(s[0] < FINE_MAX, s[1] > FINE_STOP),
                lambda s: (s[0] + 1, jnp.max(fine_step(hmat, xmat))),
                (jnp.int32(0), jnp.float32(1.0)),
            )
            store_weights(feats, xmat, scale, wh_slow, wl_slow)

    def compute(wh, wl):
        parts = [own_ref[...]] + [blocks_ref[k] for k in range(blocks_ref.shape[0])]
        out_ref[...] = corrected(
            jnp.concatenate(parts, axis=1), modes_ref[...], pack6(split3(coords_ref[...])),
            wh[...], wl[...],
        )

    good = flag[0] == 1

    @pl.when(jnp.logical_not(good))
    def _():
        compute(wh_slow, wl_slow)

    @pl.when(jnp.logical_and(good, step >= done_tiles))
    def _():
        compute(wh_ref, wl_ref)

    if done_tiles:

        @pl.when(jnp.logical_and(good, step < done_tiles))
        def _():
            out_ref[...] = done_ref[...]


def finish(done_tiles, place, done, snapshots, modes_t, ridge, blocks, coords, wh, wl, size):
    parts, count, width = blocks.shape
    times = (parts + 1) * width
    tiles = count // TILE
    fixed = lambda i, place: (0, 0)
    in_specs, args = [], ()
    if done_tiles:
        in_specs = [
            pl.BlockSpec((FEAT, TILE), lambda i, place: (0, jnp.minimum(i, done_tiles - 1)))
        ]
        args = (done,)
    in_specs += [
        pl.BlockSpec((TILE, width), lambda i, place: (place[0] * tiles + i, 0)),
        pl.BlockSpec((parts, TILE, width), lambda i, place: (0, i, 0)),
        pl.BlockSpec((R, TILE), lambda i, place: (0, place[0] * tiles + i)),
        pl.BlockSpec((R, times), fixed),
        pl.BlockSpec((FEAT, times), fixed),
        pl.BlockSpec((FEAT, times), fixed),
        pl.BlockSpec((8, 128), fixed),
        pl.BlockSpec((1, FEAT), fixed),
    ]
    args += (snapshots, blocks, modes_t, coords, wh, wl, size, ridge.reshape(1, -1))
    return pl.pallas_call(
        functools.partial(final_kernel, done_tiles),
        grid_spec=pltpu.PrefetchScalarGridSpec(
            num_scalar_prefetch=1,
            grid=(tiles,),
            in_specs=in_specs,
            out_specs=pl.BlockSpec((FEAT, TILE), lambda i, place: (0, i)),
            scratch_shapes=[
                pltpu.VMEM((FEAT, times), BF16),
                pltpu.VMEM((FEAT, times), BF16),
                pltpu.VMEM((FEAT, times), F32),
                pltpu.VMEM((times, times), F32),
                pltpu.VMEM((times, times), F32),
                pltpu.SMEM((1,), jnp.int32),
            ],
        ),
        out_shape=jax.ShapeDtypeStruct((FEAT, count), F32),
        compiler_params=pltpu.CompilerParams(vmem_limit_bytes=32 * 2**20),
        cost_estimate=pl.CostEstimate(
            flops=2 * count * times * FEAT * 3, bytes_accessed=12 * 2**20, transcendentals=0
        ),
    )(place, *args)


DONE_TILES = 3


def shards(snapshots, modes, ridge):
    nodes_total = modes.shape[0] * lax.axis_size("row")
    modes_t = modes.T
    found = exchange_and_weigh(snapshots, modes_t, ridge, nodes_total, DONE_TILES)
    blocks, coords, wh, wl, size = found[:5]
    done = found[5] if DONE_TILES else None
    place = lax.axis_index("tm").astype(jnp.int32).reshape(1)
    return finish(
        DONE_TILES, place, done, snapshots, modes_t, ridge, blocks, coords, wh, wl, size
    ).T


def solution(mesh):
    return jax.shard_map(
        shards,
        mesh=mesh,
        in_specs=(P("row", "tm"), P("row", None), P()),
        out_specs=P(("row", "tm"), None),
        check_vma=False,
    )
```

time: 2390 us -> 103 us (0.04)
  other arithmetic: 1110 us -> 0 us
  matrix products: 521 us -> 0 us
  loops' own time: 414 us -> 0 us
  waiting for transfers between devices: 284 us -> 0 us
  Pallas kernels: 0 us -> 100 us
    dot_general x1056 -> x0, other arithmetic: 683 us -> none  [the longest x528 362 us: column_step(): pivot = jnp.sqrt(jnp.dot(column, pick, precision=high))]
    dot_general x2678 -> x0, matrix products: 521 us -> none  [the longest x528 104 us: column_step(): row_here = jnp.dot(pick, lower, precision=high)]
    another operation x8 -> x0, loops' own time: 414 us -> none  [the longest x4 380 us: small_factor(): return lax.fori_loop(0, width, column_step, jnp.zeros_like(block))]
    div x529 -> x0, other arithmetic: 320 us -> none  [the longest x528 319 us: row_step(): fresh = (pick - jnp.dot(before, result, precision=high)) / pivot]
    psum x1 -> x0, waiting for transfers between devices: 237 us -> none  [shards(): summed = lax.psum(partial_sum, ('row', 'tm'))]
    pallas_call x0 -> x2, Pallas kernels: none -> 100 us  [the longest x1 57.8 us: exchange_and_weigh(): pl.pallas_call(functools.partial(main_kernel, nodes_total, done_tiles), o...]
    add x1056 -> x0, other arithmetic: 98.2 us -> none  [the longest x528 49.1 us: column_step(): return lower + scaled[:, None] * pick[None, :]]
    all_to_all x1 -> x0, waiting for transfers between devices: 46.7 us -> none  [shards(): lax.all_to_all(snapshots, 'tm', split_axis=0, concat_axis=1, tiled=True)]
where the time goes in v2:
time: 103 us; the launch traced here: 102 us
  Pallas kernels  100 us (97%)
  local copies, waits for them, and re-layouts  1.92 us (2%)
    pallas_call x1, Pallas kernels, exchange_and_weigh(): pl.pallas_call(functools.partial(main_kernel, nodes_total, done_tiles), o...  57.8 us
    pallas_call x1, Pallas kernels, finish(): pl.pallas_call(functools.partial(final_kernel, done_tiles), grid_spec=plt...  42.7 us

profile of v2, /device:TPU:1, one launch (start us, length us, event | category | flops | bytes accessed | tf_op | source)
XLA Modules:
  0.0 102.4 jit_solution(10111355998226716194)
XLA Ops:
  0.0 0.7 reshape.8.ridge_ref.refs_8_
  0.7 0.0 copy-start.1
  0.7 1.2 %copy-done.1 = f32[8192,32]{0,1:T(8,128)S(1)} copy-done((f32[8192,32]{0,1:T(8,128)S(1)}, f32[8192,32]{0,1:T(8,128)}, u32[]{:S(2)}) %copy-start.1) | copy-done | bytes 1048600
  1.9 0.0 copy-start
  1.9 0.0 copy-start.2
  1.9 57.8 %shard_map.37 = (f32[3,2048,128]{2,1,0:T(8,128)S(1)}, f32[32,512]{1,0:T(8,128)S(1)}, bf16[528,512]{1,0:T(8,128)(2,1)S(1)}, bf16[528,512]{1,0:T(8,128)(2,1)S(1)},...) custom-call(f32[8192,128]{1,0:T(8,128)} %refs_1_.1, f32[32,8192]{1,0:T(8,128)S(1)} %bitcast.3, ...), custom_call_target="tpu_custom_call" | custom-call | flops 10000000000 | bytes 16777216 | tf_op jit(solution)/shard_map/pallas_call | solution.py:317
  59.7 0.0 copy-done
  59.7 0.0 copy-done.2
  59.7 42.7 %shard_map.38 = f32[528,2048]{1,0:T(8,128)} custom-call(s32[1]{0:T(128)} %bitcast.place_ref, f32[528,1536]{1,0:T(8,128)S(1)} %get-tuple-element.11.refs_0_, f32[8192,128]{1,0:T(8,128)S(1)} %copy-done, f32[3,2048,128]{2,1,0:T(8,128)S(1)} %get-tuple-element.12.refs_2_, f32[32,8192]{1,0:T(8,128)S(1)} %bitcast.4, f32[32,512]{1,0:T(8,128)S(1)} %get-tuple-element.13.refs_4_, ...), custom_call_target="tpu_custom_call" | custom-call | flops 3321888768 | bytes 12582912 | tf_op jit(solution)/shard_map/pallas_call | solution.py:426
Async XLA Ops:
  0.7 1.2 %copy-start.1 = (f32[8192,32]{0,1:T(8,128)S(1)}, f32[8192,32]{0,1:T(8,128)}, u32[]{:S(2)}) copy-start(f32[8192,32]{0,1:T(8,128)} %param.4) | copy-start | bytes 3145732
  1.9 57.8 %copy-start = (f32[8192,128]{1,0:T(8,128)S(1)}, f32[8192,128]{1,0:T(8,128)}, u32[]{:S(2)}) copy-start(f32[8192,128]{1,0:T(8,128)} %refs_1_.1) | copy-start | bytes 12582916
  1.9 57.8 %copy-start.2 = (f32[8192,32]{0,1:T(8,128)S(1)}, f32[8192,32]{0,1:T(8,128)}, u32[]{:S(2)}) copy-start(f32[8192,32]{0,1:T(8,128)} %param.4) | copy-start | bytes 3145732

commit v3 on v2

--- a/solution.py
+++ b/solution.py
@@ -18,9 +18,10 @@
 HIGH_STOP = 0.05
 FINE_MAX = 12
 GROUP = 8
-TILE = 512
-CHUNKS = ((0, 256), (256, 256), (512, 512), (1024, 512), (1536, 512))
+TILE = 256
+CHUNKS = ((0, 256), (256, 256), (512, 512), (1024, 512), (1536, 256), (1792, 256))
 EARLY_CHUNKS = 1
+DONE = (0, 1792)
 MESH = pl.DeviceIdType.MESH
 
 
@@ -59,7 +60,7 @@
 
 
 def column_scale(ridge_ref, times):
-    row = lax.rsqrt(ridge_ref[...] * times)
+    row = lax.rsqrt(ridge_ref[...].reshape(1, FEAT) * times)
     return jnp.sum(identity(FEAT) * row, axis=1, keepdims=True)
 
 
@@ -127,15 +128,13 @@
     return dot(wh, rl, last) + dot(wl, rh, last) + dot(wh, rh, last)
 
 
-def main_kernel(nodes_total, done_tiles, snaps_ref, modes_ref, ridge_ref, *refs):
-    outs = 5 + (done_tiles > 0)
-    blocks_ref, coords_ref, wh_ref, wl_ref, size_ref = refs[:5]
-    out_ref = refs[5] if done_tiles else None
+def main_kernel(nodes_total, snaps_ref, modes_ref, ridge_hbm, *refs):
     (
-        snaps, modes_t, cross, near, far, whole, feats, hmat, xmat, packed, tiles, result,
+        blocks_ref, coords_ref, wh_ref, wl_ref, size_ref, done_ref,
+        snaps, modes_t, cross, near, far, whole, feats, hmat, xmat, packed,
         load_sem, cross_send, cross_recv, near_send, near_recv, far_send, far_recv,
-        whole_send, whole_recv, block_send, block_recv, tile_sem, result_sem,
-    ) = refs[outs:]
+        whole_send, whole_recv, block_send, block_recv, ridge_ref, ridge_sem,
+    ) = refs
     row, col = lax.axis_index("row"), lax.axis_index("tm")
     cols, planes = cross.shape[0], far.shape[0]
     plane, spot = row // GROUP, row % GROUP
@@ -188,6 +187,8 @@
 
     modes_load = pltpu.make_async_copy(modes_ref, modes_t, load_sem.at[cols])
     modes_load.start()
+    ridge_load = pltpu.make_async_copy(ridge_hbm, ridge_ref, ridge_sem)
+    ridge_load.start()
     for c in range(cols):
         load(c).start()
     barrier = pltpu.get_barrier_semaphore()
@@ -218,6 +219,7 @@
     for c in range(EARLY_CHUNKS, len(CHUNKS)):
         for k in order:
             block_copy(k, c).start()
+    ridge_load.wait()
     scale = column_scale(ridge_ref, times)
     for k in order:
         cross_copy(k).wait_recv()
@@ -254,34 +256,15 @@
         start, size = CHUNKS[t]
         for k in order:
             block_copy(k, t).wait_recv()
-        if start + size > done_tiles * TILE or (start + size) % TILE:
+        if start < DONE[0] or start >= DONE[1]:
             continue
-        tile = (start + size) // TILE - 1
-        rows = pl.ds(tile * TILE, TILE)
-        moves = [
-            pltpu.make_async_copy(
-                blocks_ref.at[k - 1, rows, :], tiles.at[k - 1], tile_sem.at[k]
-            )
-            for k in range(1, cols)
-        ]
-        for move in moves:
-            move.start()
-        for move in moves:
-            move.wait()
-        base = pl.multiple_of(col * count + tile * TILE, TILE)
-        values = jnp.concatenate(
-            [snaps[pl.ds(base, TILE), :]] + [tiles[k] for k in range(cols - 1)], axis=1
-        )
-        result[tile] = corrected(
-            values, modes_t[:, pl.ds(base, TILE)], packed[...], wh_ref[...], wl_ref[...]
-        )
-        pltpu.make_async_copy(
-            result.at[tile], out_ref.at[:, pl.ds(tile * TILE, TILE)], result_sem.at[tile]
-        ).start()
-    for tile in range(done_tiles):
-        pltpu.make_async_copy(
-            result.at[tile], out_ref.at[:, pl.ds(tile * TILE, TILE)], result_sem.at[tile]
-        ).wait()
+        base = pl.multiple_of(col * count + start, TILE)
+        values = [snaps[pl.ds(base, size), :]]
+        values += [blocks_ref[k, start : start + size, :] for k in range(cols - 1)]
+        done_ref[:, start - DONE[0] : start - DONE[0] + size] = corrected(
+            jnp.concatenate(values, axis=1), modes_t[:, pl.ds(base, size)], packed[...],
+            wh_ref[...], wl_ref[...],
+        )
     for k in range(1, cols):
         cross_copy(k).wait_send()
         for c in range(len(CHUNKS)):
@@ -293,7 +276,7 @@
         far_copy(k).wait_send()
 
 
-def exchange_and_weigh(snapshots, modes_t, ridge, nodes_total, done_tiles):
+def exchange_and_weigh(snapshots, modes_t, ridge, nodes_total):
     cols = lax.axis_size("tm")
     planes = lax.axis_size("row") // GROUP
     nodes, width = snapshots.shape
@@ -301,24 +284,20 @@
     piece = (cols, R // GROUP, width)
     dma = pltpu.SemaphoreType.DMA
     vmem = pl.BlockSpec(memory_space=pltpu.VMEM)
-    far_away = pl.BlockSpec(memory_space=pl.ANY)
+    far_away = pl.BlockSpec(memory_space=pltpu.HBM)
     shape = jax.ShapeDtypeStruct
-    out_shape = [
-        shape((cols - 1, count, width), F32),
-        shape((R, times), F32),
-        shape((FEAT, times), BF16),
-        shape((FEAT, times), BF16),
-        shape((8, 128), F32),
-    ]
-    out_specs = [far_away, vmem, vmem, vmem, vmem]
-    if done_tiles:
-        out_shape.append(shape((FEAT, done_tiles * TILE), F32))
-        out_specs.append(far_away)
     return pl.pallas_call(
-        functools.partial(main_kernel, nodes_total, done_tiles),
-        out_shape=out_shape,
-        in_specs=[far_away, far_away, vmem],
-        out_specs=out_specs,
+        functools.partial(main_kernel, nodes_total),
+        out_shape=[
+            shape((cols - 1, count, width), F32),
+            shape((R, times), F32),
+            shape((FEAT, times), BF16),
+            shape((FEAT, times), BF16),
+            shape((8, 128), F32),
+            shape((FEAT, DONE[1] - DONE[0]), F32),
+        ],
+        in_specs=[far_away] * 3,
+        out_specs=[vmem] * 6,
         scratch_shapes=[
             pltpu.VMEM((nodes, width), F32),
             pltpu.VMEM((R, nodes), F32),
@@ -330,136 +309,140 @@
             pltpu.VMEM((times, times), F32),
             pltpu.VMEM((times, times), F32),
             pltpu.VMEM((6 * R, times), BF16),
-            pltpu.VMEM((cols - 1, TILE, width), F32),
-            pltpu.VMEM((max(done_tiles, 1), FEAT, TILE), F32),
             dma((cols + 1,)),
             dma((cols,)), dma((cols,)),
             dma((GROUP,)), dma((GROUP,)),
             dma((planes,)), dma((planes,)),
             dma((GROUP,)), dma((GROUP,)),
             dma((cols, len(CHUNKS))), dma((cols, len(CHUNKS))),
-            dma((cols,)),
-            dma((max(done_tiles, 1),)),
+            pltpu.VMEM((FEAT,), F32), dma,
         ],
         compiler_params=pltpu.CompilerParams(
             collective_id=0, has_side_effects=True, vmem_limit_bytes=44 * 2**20
         ),
         cost_estimate=pl.CostEstimate(flops=10**10, bytes_accessed=2**24, transcendentals=0),
-    )(snapshots, modes_t, ridge.reshape(1, -1))
-
-
-def final_kernel(done_tiles, place_ref, *refs):
-    if done_tiles:
-        done_ref, refs = refs[0], refs[1:]
-    own_ref, blocks_ref, modes_ref, coords_ref, wh_ref, wl_ref, size_ref, ridge_ref = refs[:8]
-    out_ref, wh_slow, wl_slow, feats, hmat, xmat, flag = refs[8:]
-    step = pl.program_id(0)
+    )(snapshots, modes_t, ridge)
+
+
+def final_kernel(
+    snaps_ref, modes_ref, ridge_ref, blocks_ref, coords_ref, wh_ref, wl_ref, size_ref, done_ref,
+    *refs,
+):
+    early, refs = refs[:-12], refs[-12:]
+    (
+        out_ref, own, modes_t, result, wh_slow, wl_slow, feats, hmat, xmat,
+        load_sem, done_sem, result_sem,
+    ) = refs
     times = hmat.shape[0]
-
-    @pl.when(step == 0)
+    parts, count, _ = blocks_ref.shape
+    tiles = count // TILE
+    first = lax.axis_index("tm") * count
+    rest = [t for t in range(tiles) if not DONE[0] <= t * TILE < DONE[1]]
+
+    def moves(slot, tile):
+        rows = pl.ds(pl.multiple_of(first + tile * TILE, TILE), TILE)
+        return (
+            pltpu.make_async_copy(snaps_ref.at[rows, :], own.at[slot], load_sem.at[slot, 0]),
+            pltpu.make_async_copy(modes_ref.at[:, rows], modes_t.at[slot], load_sem.at[slot, 1]),
+        )
+
+    def store(slot, tile):
+        columns = pl.ds(pl.multiple_of(tile * TILE, TILE), TILE)
+        return pltpu.make_async_copy(
+            result.at[slot], out_ref.at[:, columns], result_sem.at[slot]
+        )
+
+    def compute(slot, tile, wh, wl):
+        rows = pl.ds(pl.multiple_of(tile * TILE, TILE), TILE)
+        if early and isinstance(tile, int) and tile == 0:
+            others = [block[...] for block in early]
+        else:
+            others = [blocks_ref[k, rows, :] for k in range(parts)]
+        result[slot] = corrected(
+            jnp.concatenate([own[slot]] + others, axis=1), modes_t[slot],
+            pack6(split3(coords_ref[...])), wh[...], wl[...],
+        )
+
+    good = jnp.max(size_ref[...]) <= FINE_STOP
+
+    @pl.when(good)
     def _():
-        good = jnp.max(size_ref[...]) <= FINE_STOP
-        flag[0] = good.astype(jnp.int32)
-
-        @pl.when(jnp.logical_not(good))
-        def _():
-            scale = column_scale(ridge_ref, times)
-            fill_feats(coords_ref[...], scale, feats)
-            rho = jnp.max(first_guess(feats, hmat, xmat))
-            lax.while_loop(
-                lambda r: r > HIGH_STOP, lambda r: high_step(hmat, xmat, r), rho
-            )
-
-            lax.while_loop(
-                lambda s: jnp.logical_and(s[0] < FINE_MAX, s[1] > FINE_STOP),
-                lambda s: (s[0] + 1, jnp.max(fine_step(hmat, xmat))),
-                (jnp.int32(0), jnp.float32(1.0)),
-            )
-            store_weights(feats, xmat, scale, wh_slow, wl_slow)
-
-    def compute(wh, wl):
-        parts = [own_ref[...]] + [blocks_ref[k] for k in range(blocks_ref.shape[0])]
-        out_ref[...] = corrected(
-            jnp.concatenate(parts, axis=1), modes_ref[...], pack6(split3(coords_ref[...])),
-            wh[...], wl[...],
-        )
-
-    good = flag[0] == 1
+        copy = pltpu.make_async_copy(
+            done_ref, out_ref.at[:, pl.ds(DONE[0], DONE[1] - DONE[0])], done_sem
+        )
+        for slot, tile in enumerate(rest):
+            for move in moves(slot, tile):
+                move.start()
+        copy.start()
+        for slot, tile in enumerate(rest):
+            for move in moves(slot, tile):
+                move.wait()
+            compute(slot, tile, wh_ref, wl_ref)
+            store(slot, tile).start()
+        for slot, tile in enumerate(rest):
+            store(slot, tile).wait()
+        copy.wait()
 
     @pl.when(jnp.logical_not(good))
     def _():
-        compute(wh_slow, wl_slow)
-
-    @pl.when(jnp.logical_and(good, step >= done_tiles))
-    def _():
-        compute(wh_ref, wl_ref)
-
-    if done_tiles:
-
-        @pl.when(jnp.logical_and(good, step < done_tiles))
-        def _():
-            out_ref[...] = done_ref[...]
-
-
-def finish(done_tiles, place, done, snapshots, modes_t, ridge, blocks, coords, wh, wl, size):
+        scale = column_scale(ridge_ref, times)
+        fill_feats(coords_ref[...], scale, feats)
+        rho = jnp.max(first_guess(feats, hmat, xmat))
+        lax.while_loop(lambda r: r > HIGH_STOP, lambda r: high_step(hmat, xmat, r), rho)
+        lax.while_loop(
+            lambda s: jnp.logical_and(s[0] < FINE_MAX, s[1] > FINE_STOP),
+            lambda s: (s[0] + 1, jnp.max(fine_step(hmat, xmat))),
+            (jnp.int32(0), jnp.float32(1.0)),
+        )
+        store_weights(feats, xmat, scale, wh_slow, wl_slow)
+
+        def whole_tile(tile):
+            for move in moves(0, tile):
+                move.start()
+            for move in moves(0, tile):
+                move.wait()
+            compute(0, tile, wh_slow, wl_slow)
+            store(0, tile).start()
+            store(0, tile).wait()
+
+        whole_tile(0)
+        lax.fori_loop(1, tiles, lambda tile, _: whole_tile(tile), None)
+
+
+def finish(snapshots, modes_t, ridge, blocks, coords, wh, wl, size, done, early):
     parts, count, width = blocks.shape
     times = (parts + 1) * width
-    tiles = count // TILE
-    fixed = lambda i, place: (0, 0)
-    in_specs, args = [], ()
-    if done_tiles:
-        in_specs = [
-            pl.BlockSpec((FEAT, TILE), lambda i, place: (0, jnp.minimum(i, done_tiles - 1)))
-        ]
-        args = (done,)
-    in_specs += [
-        pl.BlockSpec((TILE, width), lambda i, place: (place[0] * tiles + i, 0)),
-        pl.BlockSpec((parts, TILE, width), lambda i, place: (0, i, 0)),
-        pl.BlockSpec((R, TILE), lambda i, place: (0, place[0] * tiles + i)),
-        pl.BlockSpec((R, times), fixed),
-        pl.BlockSpec((FEAT, times), fixed),
-        pl.BlockSpec((FEAT, times), fixed),
-        pl.BlockSpec((8, 128), fixed),
-        pl.BlockSpec((1, FEAT), fixed),
-    ]
-    args += (snapshots, blocks, modes_t, coords, wh, wl, size, ridge.reshape(1, -1))
+    slots = (count - DONE[1] + DONE[0]) // TILE
+    dma = pltpu.SemaphoreType.DMA
+    vmem = pl.BlockSpec(memory_space=pltpu.VMEM)
+    far_away = pl.BlockSpec(memory_space=pltpu.HBM)
     return pl.pallas_call(
-        functools.partial(final_kernel, done_tiles),
-        grid_spec=pltpu.PrefetchScalarGridSpec(
-            num_scalar_prefetch=1,
-            grid=(tiles,),
-            in_specs=in_specs,
-            out_specs=pl.BlockSpec((FEAT, TILE), lambda i, place: (0, i)),
-            scratch_shapes=[
-                pltpu.VMEM((FEAT, times), BF16),
-                pltpu.VMEM((FEAT, times), BF16),
-                pltpu.VMEM((FEAT, times), F32),
-                pltpu.VMEM((times, times), F32),
-                pltpu.VMEM((times, times), F32),
-                pltpu.SMEM((1,), jnp.int32),
-            ],
-        ),
+        final_kernel,
         out_shape=jax.ShapeDtypeStruct((FEAT, count), F32),
-        compiler_params=pltpu.CompilerParams(vmem_limit_bytes=32 * 2**20),
-        cost_estimate=pl.CostEstimate(
-            flops=2 * count * times * FEAT * 3, bytes_accessed=12 * 2**20, transcendentals=0
-        ),
-    )(place, *args)
-
-
-DONE_TILES = 3
+        in_specs=[far_away, far_away] + [vmem] * (7 + len(early)),
+        out_specs=far_away,
+        scratch_shapes=[
+            pltpu.VMEM((slots, TILE, width), F32),
+            pltpu.VMEM((slots, R, TILE), F32),
+            pltpu.VMEM((slots, FEAT, TILE), F32),
+            pltpu.VMEM((FEAT, times), BF16),
+            pltpu.VMEM((FEAT, times), BF16),
+            pltpu.VMEM((FEAT, times), F32),
+            pltpu.VMEM((times, times), F32),
+            pltpu.VMEM((times, times), F32),
+            dma((slots, 2)), dma, dma((slots,)),
+        ],
+        compiler_params=pltpu.CompilerParams(vmem_limit_bytes=36 * 2**20),
+        cost_estimate=pl.CostEstimate(flops=10**9, bytes_accessed=2**23, transcendentals=0),
+    )(snapshots, modes_t, ridge, blocks, coords, wh, wl, size, done, *early)
 
 
 def shards(snapshots, modes, ridge):
     nodes_total = modes.shape[0] * lax.axis_size("row")
     modes_t = modes.T
-    found = exchange_and_weigh(snapshots, modes_t, ridge, nodes_total, DONE_TILES)
-    blocks, coords, wh, wl, size = found[:5]
-    done = found[5] if DONE_TILES else None
-    place = lax.axis_index("tm").astype(jnp.int32).reshape(1)
-    return finish(
-        DONE_TILES, place, done, snapshots, modes_t, ridge, blocks, coords, wh, wl, size
-    ).T
+    early = []
+    found = exchange_and_weigh(snapshots, modes_t, ridge, nodes_total)
+    return finish(snapshots, modes_t, ridge, *found, early).T
 
 
 def solution(mesh):

time: 103 us -> 108 us (1.049)
  Pallas kernels: 100 us -> 105 us
    pallas_call x2, Pallas kernels: 100 us -> 105 us  [the longest x1 57.8 us: exchange_and_weigh(): pl.pallas_call(functools.partial(main_kernel, nodes_total), out_shape=[sh...]
where the time goes in v3:
time: 108 us
  Pallas kernels  105 us (97%)
  local copies, waits for them, and re-layouts  1.92 us (2%)
    pallas_call x1, Pallas kernels, exchange_and_weigh(): pl.pallas_call(functools.partial(main_kernel, nodes_total), out_shape=[sh...  57.8 us
    pallas_call x1, Pallas kernels, finish(): pl.pallas_call(final_kernel, out_shape=jax.ShapeDtypeStruct((FEAT, count)...  47.7 us

profile of v3, /device:TPU:1, one launch (start us, length us, event | category | flops | bytes accessed | tf_op | source)
XLA Modules:
  0.0 107.6 jit_solution(4674155488923840711)
XLA Ops:
  0.0 0.0 copy-start.1
  0.0 1.2 %copy-done.1 = f32[8192,32]{0,1:T(8,128)S(1)} copy-done((f32[8192,32]{0,1:T(8,128)S(1)}, f32[8192,32]{0,1:T(8,128)}, u32[]{:S(2)}) %copy-start.1) | copy-done | bytes 1048600
  1.2 0.0 copy-start.3
  1.2 0.7 copy-done.3
  1.9 0.0 copy-start
  1.9 0.0 copy-start.2
  1.9 57.8 %shard_map.37 = (f32[3,2048,128]{2,1,0:T(8,128)S(1)}, f32[32,512]{1,0:T(8,128)S(1)}, bf16[528,512]{1,0:T(8,128)(2,1)S(1)}, bf16[528,512]{1,0:T(8,128)(2,1)S(1)},...) custom-call(f32[8192,128]{1,0:T(8,128)} %snaps_ref.3, f32[32,8192]{1,0:T(8,128)S(1)} %bitcast.2, f32[528]{0:T(1024)S(1)} %copy-done.3), custom_call_target="tpu_custom_call" | custom-call | flops 10000000000 | bytes 16777216 | tf_op jit(solution)/shard_map/pallas_call | solution.py:289
  59.7 0.0 copy-done
  59.8 0.0 copy-done.2
  59.8 47.7 %shard_map.38 = f32[528,2048]{1,0:T(8,128)} custom-call(f32[8192,128]{1,0:T(8,128)S(1)} %copy-done, f32[32,8192]{1,0:T(8,128)S(1)} %bitcast.3, f32[528]{0:T(1024)S(1)} %copy-done.3, f32[3,2048,128]{2,1,0:T(8,128)S(1)} %get-tuple-element.11.blocks_ref, f32[32,512]{1,0:T(8,128)S(1)} %get-tuple-element.12.coords_ref, ...), custom_call_target="tpu_custom_call" | custom-call | flops 1000000000 | bytes 8388608 | tf_op jit(solution)/shard_map/pallas_call | solution.py:419
Async XLA Ops:
  0.0 1.2 %copy-start.1 = (f32[8192,32]{0,1:T(8,128)S(1)}, f32[8192,32]{0,1:T(8,128)}, u32[]{:S(2)}) copy-start(f32[8192,32]{0,1:T(8,128)} %param.4) | copy-start | bytes 3145732
  1.2 0.7 copy-start.3
  1.9 57.8 %copy-start = (f32[8192,128]{1,0:T(8,128)S(1)}, f32[8192,128]{1,0:T(8,128)}, u32[]{:S(2)}) copy-start(f32[8192,128]{1,0:T(8,128)} %snaps_ref.3) | copy-start | bytes 12582916
  1.9 57.8 %copy-start.2 = (f32[8192,32]{0,1:T(8,128)S(1)}, f32[8192,32]{0,1:T(8,128)}, u32[]{:S(2)}) copy-start(f32[8192,32]{0,1:T(8,128)} %param.4) | copy-start | bytes 3145732

commit v4 on v3

--- a/solution.py
+++ b/solution.py
@@ -18,10 +18,10 @@
 HIGH_STOP = 0.05
 FINE_MAX = 12
 GROUP = 8
-TILE = 256
-CHUNKS = ((0, 256), (256, 256), (512, 512), (1024, 512), (1536, 256), (1792, 256))
+TILE = 128
+CHUNKS = ((0, 256), (256, 256), (512, 512), (1024, 512), (1536, 256), (1792, 128), (1920, 128))
 EARLY_CHUNKS = 1
-DONE = (0, 1792)
+DONE = (0, 1920)
 MESH = pl.DeviceIdType.MESH
 
 
@@ -185,17 +185,17 @@
         rows = pl.ds(c * count, count)
         return pltpu.make_async_copy(snaps_ref.at[rows, :], snaps.at[rows, :], load_sem.at[c])
 
+    barrier = pltpu.get_barrier_semaphore()
+    peers = [far_peer(k) for k in range(1, planes)] + [cross_peer(k) for k in range(1, cols)]
+    peers += [near_peer(k) for k in range(1, GROUP)]
+    for peer in peers:
+        pl.semaphore_signal(barrier, inc=1, device_id=peer, device_id_type=MESH)
     modes_load = pltpu.make_async_copy(modes_ref, modes_t, load_sem.at[cols])
     modes_load.start()
     ridge_load = pltpu.make_async_copy(ridge_hbm, ridge_ref, ridge_sem)
     ridge_load.start()
     for c in range(cols):
         load(c).start()
-    barrier = pltpu.get_barrier_semaphore()
-    peers = [cross_peer(k) for k in range(1, cols)]
-    peers += [near_peer(k) for k in range(1, GROUP)] + [far_peer(k) for k in range(1, planes)]
-    for peer in peers:
-        pl.semaphore_signal(barrier, inc=1, device_id=peer, device_id_type=MESH)
     pl.semaphore_wait(barrier, len(peers))
 
     order = [1, cols - 1] + list(range(2, cols - 1))
@@ -363,25 +363,22 @@
             pack6(split3(coords_ref[...])), wh[...], wl[...],
         )
 
+    copy = pltpu.make_async_copy(
+        done_ref, out_ref.at[:, pl.ds(DONE[0], DONE[1] - DONE[0])], done_sem
+    )
+    for slot, tile in enumerate(rest):
+        for move in moves(slot, tile):
+            move.start()
+    copy.start()
     good = jnp.max(size_ref[...]) <= FINE_STOP
-
-    @pl.when(good)
-    def _():
-        copy = pltpu.make_async_copy(
-            done_ref, out_ref.at[:, pl.ds(DONE[0], DONE[1] - DONE[0])], done_sem
-        )
-        for slot, tile in enumerate(rest):
-            for move in moves(slot, tile):
-                move.start()
-        copy.start()
-        for slot, tile in enumerate(rest):
-            for move in moves(slot, tile):
-                move.wait()
-            compute(slot, tile, wh_ref, wl_ref)
-            store(slot, tile).start()
-        for slot, tile in enumerate(rest):
-            store(slot, tile).wait()
-        copy.wait()
+    for slot, tile in enumerate(rest):
+        for move in moves(slot, tile):
+            move.wait()
+        compute(slot, tile, wh_ref, wl_ref)
+        store(slot, tile).start()
+    for slot, tile in enumerate(rest):
+        store(slot, tile).wait()
+    copy.wait()
 
     @pl.when(jnp.logical_not(good))
     def _():

time: 108 us -> 120 us (1.11)
  Pallas kernels: 105 us -> 118 us
    pallas_call x1, Pallas kernels: 47.7 us -> 60.2 us  [finish(): pl.pallas_call(final_kernel, out_shape=jax.ShapeDtypeStruct((FEAT, count)...]
where the time goes in v4:
time: 120 us
  Pallas kernels  118 us (98%)
  local copies, waits for them, and re-layouts  1.92 us (2%)
    pallas_call x1, Pallas kernels, finish(): pl.pallas_call(final_kernel, out_shape=jax.ShapeDtypeStruct((FEAT, count)...  60.2 us
    pallas_call x1, Pallas kernels, exchange_and_weigh(): pl.pallas_call(functools.partial(main_kernel, nodes_total), out_shape=[sh...  57.4 us

profile of v4, /device:TPU:1, one launch (start us, length us, event | category | flops | bytes accessed | tf_op | source)
XLA Modules:
  0.0 119.7 jit_solution(251370421666692611)
XLA Ops:
  0.0 0.0 copy-start.1
  0.0 1.2 %copy-done.1 = f32[8192,32]{0,1:T(8,128)S(1)} copy-done((f32[8192,32]{0,1:T(8,128)S(1)}, f32[8192,32]{0,1:T(8,128)}, u32[]{:S(2)}) %copy-start.1) | copy-done | bytes 1048600
  1.2 0.0 copy-start.3
  1.2 0.7 copy-done.3
  1.9 0.0 copy-start
  1.9 0.0 copy-start.2
  1.9 57.4 %shard_map.37 = (f32[3,2048,128]{2,1,0:T(8,128)S(1)}, f32[32,512]{1,0:T(8,128)S(1)}, bf16[528,512]{1,0:T(8,128)(2,1)S(1)}, bf16[528,512]{1,0:T(8,128)(2,1)S(1)},...) custom-call(f32[8192,128]{1,0:T(8,128)} %snaps_ref.3, f32[32,8192]{1,0:T(8,128)S(1)} %bitcast.2, f32[528]{0:T(1024)S(1)} %copy-done.3), custom_call_target="tpu_custom_call" | custom-call | flops 10000000000 | bytes 16777216 | tf_op jit(solution)/shard_map/pallas_call | solution.py:289
  59.3 0.0 copy-done
  59.3 0.0 copy-done.2
  59.3 60.2 %shard_map.38 = f32[528,2048]{1,0:T(8,128)} custom-call(f32[8192,128]{1,0:T(8,128)S(1)} %copy-done, f32[32,8192]{1,0:T(8,128)S(1)} %bitcast.3, f32[528]{0:T(1024)S(1)} %copy-done.3, f32[3,2048,128]{2,1,0:T(8,128)S(1)} %get-tuple-element.11.blocks_ref, f32[32,512]{1,0:T(8,128)S(1)} %get-tuple-element.12.coords_ref, ...), custom_call_target="tpu_custom_call" | custom-call | flops 1000000000 | bytes 8388608 | tf_op jit(solution)/shard_map/pallas_call | solution.py:416
Async XLA Ops:
  0.0 1.2 %copy-start.1 = (f32[8192,32]{0,1:T(8,128)S(1)}, f32[8192,32]{0,1:T(8,128)}, u32[]{:S(2)}) copy-start(f32[8192,32]{0,1:T(8,128)} %param.4) | copy-start | bytes 3145732
  1.2 0.7 copy-start.3
  1.9 57.4 %copy-start = (f32[8192,128]{1,0:T(8,128)S(1)}, f32[8192,128]{1,0:T(8,128)}, u32[]{:S(2)}) copy-start(f32[8192,128]{1,0:T(8,128)} %snaps_ref.3) | copy-start | bytes 12582916
  1.9 57.4 %copy-start.2 = (f32[8192,32]{0,1:T(8,128)S(1)}, f32[8192,32]{0,1:T(8,128)}, u32[]{:S(2)}) copy-start(f32[8192,32]{0,1:T(8,128)} %param.4) | copy-start | bytes 3145732

commit v5 on v4

--- a/solution.py
+++ b/solution.py
@@ -20,7 +20,7 @@
 GROUP = 8
 TILE = 128
 CHUNKS = ((0, 256), (256, 256), (512, 512), (1024, 512), (1536, 256), (1792, 128), (1920, 128))
-EARLY_CHUNKS = 1
+EARLY_CHUNKS = 0
 DONE = (0, 1920)
 MESH = pl.DeviceIdType.MESH
 
@@ -196,13 +196,8 @@
     ridge_load.start()
     for c in range(cols):
         load(c).start()
-    pl.semaphore_wait(barrier, len(peers))
 
     order = [1, cols - 1] + list(range(2, cols - 1))
-    for c in range(EARLY_CHUNKS):
-        for k in order:
-            block_copy(k, c).start()
-
     modes_load.wait()
     total = jnp.zeros((2 * R, snaps.shape[1]), F32)
     for c in range(cols):
@@ -214,6 +209,7 @@
     share = R // GROUP
     for s in range(GROUP):
         cross[0, s] = mine[share * s : share * (s + 1), :]
+    pl.semaphore_wait(barrier, len(peers))
     for k in order:
         cross_copy(k).start()
     for c in range(EARLY_CHUNKS, len(CHUNKS)):

time: 120 us -> 120 us (level)
  no operation moved by 1% of the time
where the time goes in v5:
time: 120 us; the launch traced here: 119 us
  Pallas kernels  117 us (98%)
  local copies, waits for them, and re-layouts  1.92 us (2%)
    pallas_call x1, Pallas kernels, finish(): pl.pallas_call(final_kernel, out_shape=jax.ShapeDtypeStruct((FEAT, count)...  60.2 us
    pallas_call x1, Pallas kernels, exchange_and_weigh(): pl.pallas_call(functools.partial(main_kernel, nodes_total), out_shape=[sh...  57.1 us

profile of v5, /device:TPU:1, one launch (start us, length us, event | category | flops | bytes accessed | tf_op | source)
XLA Modules:
  0.0 119.5 jit_solution(18216684521152130366)
XLA Ops:
  0.0 0.0 copy-start.1
  0.0 1.2 %copy-done.1 = f32[8192,32]{0,1:T(8,128)S(1)} copy-done((f32[8192,32]{0,1:T(8,128)S(1)}, f32[8192,32]{0,1:T(8,128)}, u32[]{:S(2)}) %copy-start.1) | copy-done | bytes 1048600
  1.2 0.0 copy-start.3
  1.2 0.7 copy-done.3
  1.9 0.0 copy-start
  1.9 0.0 copy-start.2
  1.9 57.1 %shard_map.37 = (f32[3,2048,128]{2,1,0:T(8,128)S(1)}, f32[32,512]{1,0:T(8,128)S(1)}, bf16[528,512]{1,0:T(8,128)(2,1)S(1)}, bf16[528,512]{1,0:T(8,128)(2,1)S(1)},...) custom-call(f32[8192,128]{1,0:T(8,128)} %snaps_ref.3, f32[32,8192]{1,0:T(8,128)S(1)} %bitcast.2, f32[528]{0:T(1024)S(1)} %copy-done.3), custom_call_target="tpu_custom_call" | custom-call | flops 10000000000 | bytes 16777216 | tf_op jit(solution)/shard_map/pallas_call | solution.py:285
  59.1 0.0 copy-done
  59.1 0.0 copy-done.2
  59.1 60.2 %shard_map.38 = f32[528,2048]{1,0:T(8,128)} custom-call(f32[8192,128]{1,0:T(8,128)S(1)} %copy-done, f32[32,8192]{1,0:T(8,128)S(1)} %bitcast.3, f32[528]{0:T(1024)S(1)} %copy-done.3, f32[3,2048,128]{2,1,0:T(8,128)S(1)} %get-tuple-element.11.blocks_ref, f32[32,512]{1,0:T(8,128)S(1)} %get-tuple-element.12.coords_ref, ...), custom_call_target="tpu_custom_call" | custom-call | flops 1000000000 | bytes 8388608 | tf_op jit(solution)/shard_map/pallas_call | solution.py:412
Async XLA Ops:
  0.0 1.2 %copy-start.1 = (f32[8192,32]{0,1:T(8,128)S(1)}, f32[8192,32]{0,1:T(8,128)}, u32[]{:S(2)}) copy-start(f32[8192,32]{0,1:T(8,128)} %param.4) | copy-start | bytes 3145732
  1.2 0.7 copy-start.3
  1.9 57.2 %copy-start = (f32[8192,128]{1,0:T(8,128)S(1)}, f32[8192,128]{1,0:T(8,128)}, u32[]{:S(2)}) copy-start(f32[8192,128]{1,0:T(8,128)} %snaps_ref.3) | copy-start | bytes 12582916
  1.9 57.2 %copy-start.2 = (f32[8192,32]{0,1:T(8,128)S(1)}, f32[8192,32]{0,1:T(8,128)}, u32[]{:S(2)}) copy-start(f32[8192,32]{0,1:T(8,128)} %param.4) | copy-start | bytes 3145732
